TPU v7x, 128 devices: a whole 4x4x4 slice. The times are simulated.
128 devices in a mesh: yz: 32 (over z, y, core), sp: 4 (over x).
Axes of the slice: x: 4, y: 4, z: 4, core: 2. Of those that a mesh axis runs over, the one named last changes fastest.
Arguments:
- field: float32 [24, 256, 256, 256], P('sp', 'yz'), may hold values from -48 to 48
- start: float32 [256, 96], replicated, may hold values from -6 to 6
Outputs:
- core_block: float32 [24, 96, 256, 256], P('sp', None, 'yz')
- factor: float32 [256, 96], replicated
All inputs are finite; a program needn't handle non-finite values.
Results may differ from a plain program's by a relative error of at most 0.00027.
Values sent between devices are 32-bit elements; how exact they have to be, the bound alone decides.
No kernel may reach another device: no remote copies, remote signals or barrier semaphores. Data moves between devices by JAX's collectives and lax.ppermute only.
A program may use at most 128 MiB of HBM per device.

v0:
```python
import jax
import jax.numpy as jnp
from jax import lax
from jax.sharding import PartitionSpec as P

HIGH = lax.Precision.HIGHEST


def orth(matrix):
    square = jnp.dot(matrix.T, matrix, precision=HIGH)
    lower = jnp.linalg.cholesky(square)
    return lax.linalg.triangular_solve(lower, matrix, left_side=False, lower=True, transpose_a=True)


def gram_items(block):
    partial_gram = jnp.einsum("sxyz,swyz->sxw", block, block, precision=HIGH)
    return (block, partial_gram)


def local(field, start):
    fibres, partials = gram_items(
        lax.all_to_all(field, "yz", split_axis=2, concat_axis=1, tiled=True)
    )
    local_gram = jnp.sum(partials, axis=0)
    gram = lax.psum(local_gram, ("yz", "sp"))
    first = orth(jnp.dot(gram, start, precision=HIGH))
    factor = orth(jnp.dot(gram, first, precision=HIGH))
    core_block = jnp.einsum("xr,sxyz->sryz", factor, fibres, precision=HIGH)
    return (core_block, factor)


def solution(mesh):
    in_specs = (P("sp", "yz", None, None), P())
    out_specs = (P("sp", None, "yz", None), P())
    return jax.shard_map(local, mesh=mesh, in_specs=in_specs, out_specs=out_specs, check_vma=False)
```

profile of v0, /device:TPU:1, one launch (start us, length us, event | category | flops | bytes accessed | tf_op | source)
XLA Modules:
  0.0 392.7 jit_solution(5293614947900499413)
XLA Ops:
  7.2 0.0 all-reduce.2.cloned.1.call-start
  7.2 16.4 %copy.9 = f32[6,8,256,256]{3,1,0,2:T(8,128)} copy(f32[6,8,256,256]{3,2,1,0:T(8,128)} %param.5) | data formatting | bytes 25165824 | tf_op args[0]
  23.7 150.4 %all_to_all.18 = f32[6,8,256,256]{3,1,0,2:T(8,128)S(1)} all-to-all(f32[6,8,256,256]{3,1,0,2:T(8,128)} %copy.9), channel_id=1, replica_groups=mesh['yz'=32,'sp'=4] {'yz'}, dimensions={2} | all-to-all | bytes 25165824 | tf_op jit(solution)/shard_map/all_to_all | solution.py:22
  174.0 4.6 %copy-done.1 = f32[6,8,256,256]{3,1,0,2:T(8,128)} copy-done((f32[6,8,256,256]{3,1,0,2:T(8,128)}, f32[6,8,256,256]{3,1,0,2:T(8,128)S(1)}, u32[]{:S(2)}) %copy-start.1) | copy-done | bytes 12582936
  178.6 10.9 %convolution_bitcast_fusion = f32[256,256]{1,0:T(8,128)} fusion(f32[6,8,32,8,256]{4,1,0,3,2:T(8,128)S(1)} %bitcast.51), kind=kOutput, calls=%fused_computation.4 | convolution fusion | flops 9663676416 | bytes 12845056 | tf_op jit(solution)/shard_map/sxyz,swyz->sxw/dot_general | solution.py:16
  189.5 141.4 %all-reduce.2.cloned.1.call-done = f32[256,256]{1,0:T(8,128)} async-done(((f32[256,256]{1,0:T(8,128)}), f32[256,256]{1,0:T(8,128)}) %all-reduce.2.cloned.1.call-update) | async-done | bytes 262160 | tf_op jit(solution)/shard_map/psum | solution.py:25
  331.0 1.3 fusion.15
  332.3 0.2 fusion.16
  332.6 0.1 copy.11
  332.7 9.0 %cholesky.44 = f32[96,96]{1,0:T(8,128)S(1)} custom-call(f32[96,96]{1,0:T(8,128)S(1)} %fusion.12), custom_call_target="Cholesky" | custom-call | tf_op jit(solution)/shard_map/jit(cholesky)/cholesky | solution.py:11
  341.7 0.6 compare_reduce_fusion.1
  342.3 0.7 fusion.6
  343.0 7.4 %custom-call.6 = f32[1,96,96]{1,2,0:T(8,128)S(1)} custom-call(f32[1,96,96]{2,1,0:T(8,128)S(1)} %fusion.6), custom_call_target="InvertDiagBlocksLowerTriangular" | custom-call | tf_op jit(solution)/shard_map/triangular_solve/custom-call.0 | solution.py:12
  350.3 0.3 convolution_bitcast_fusion.1
  350.6 1.3 fusion.17
  352.0 0.2 fusion.18
  352.2 0.1 copy.12
  352.3 8.8 %cholesky.55 = f32[96,96]{1,0:T(8,128)S(1)} custom-call(f32[96,96]{1,0:T(8,128)S(1)} %fusion.10), custom_call_target="Cholesky" | custom-call | tf_op jit(solution)/shard_map/jit(cholesky)/cholesky | solution.py:11
  361.2 0.6 compare_reduce_fusion
  361.8 0.7 fusion.7
  362.5 7.4 %custom-call.7 = f32[1,96,96]{1,2,0:T(8,128)S(1)} custom-call(f32[1,96,96]{2,1,0:T(8,128)S(1)} %fusion.7), custom_call_target="InvertDiagBlocksLowerTriangular" | custom-call | tf_op jit(solution)/shard_map/triangular_solve/custom-call.0 | solution.py:12
  369.8 0.3 fusion.8
  370.1 10.8 %fusion.2 = f32[6,96,8,256]{3,1,2,0:T(8,128)S(1)} fusion(f32[96,256]{1,0:T(8,128)S(1)} %fusion.8, f32[6,8,32,8,256]{4,1,0,3,2:T(8,128)} %bitcast.52), kind=kOutput, calls=%fused_computation.3 | convolution fusion | flops 3623878656 | bytes 17399808 | tf_op jit(solution)/shard_map/xr,sxyz->sryz/dot_general | solution.py:28
  380.9 4.9 %copy.14 = f32[6,96,8,256]{3,2,1,0:T(8,128)} copy(f32[6,96,8,256]{3,1,2,0:T(8,128)S(1)} %fusion.2) | data formatting | bytes 9437184
  (10 shorter events, 0.1 us)
Async XLA Ops:
  7.2 323.8 %copy-start = (f32[256,96]{0,1:T(8,128)S(1)}, f32[256,96]{0,1:T(8,128)}, u32[]{:S(2)}) copy-start(f32[256,96]{0,1:T(8,128)} %param.6) | copy-start | bytes 294916
  7.2 323.8 %all-reduce.2.cloned.1.call-start = ((), (), s32[]{:S(2)}) async-start(), calls=%async_computation.1 | async-start | bytes 524288 | tf_op jit(solution)/shard_map/psum | solution.py:25
  174.0 4.6 %copy-start.1 = (f32[6,8,256,256]{3,1,0,2:T(8,128)}, f32[6,8,256,256]{3,1,0,2:T(8,128)S(1)}, u32[]{:S(2)}) copy-start(f32[6,8,256,256]{3,1,0,2:T(8,128)S(1)} %all_to_all.18) | copy-start | bytes 37748740
  370.1 15.7 %copy-start.2 = (f32[96,256]{1,0:T(8,128)}, f32[96,256]{1,0:T(8,128)S(1)}, u32[]{:S(2)}) copy-start(f32[96,256]{1,0:T(8,128)S(1)} %fusion.8) | copy-start | bytes 294916
Sparse Core Ops, SparseCore 0:
  189.7 141.2 all-reduce.1
where the time goes:
time: 393 us
  blocking collectives  150 us (38%)
  waiting for transfers between devices  141 us (36%)
  other arithmetic  35.1 us (9%)
  local copies, waits for them, and re-layouts  26 us (7%)
  matrix products  25.4 us (6%)
  between operations  14.2 us (4%)
    all_to_all x1, blocking collectives, local(): lax.all_to_all(field, 'yz', split_axis=2, concat_axis=1, tiled=True)  150 us
    psum x1, waiting for transfers between devices, local(): gram = lax.psum(local_gram, ('yz', 'sp'))  141 us
    unnamed x8, local copies, waits for them, and re-layouts  25.9 us
    another operation x6, other arithmetic, orth(): lower = jnp.linalg.cholesky(square)  19.1 us
    another operation x4, other arithmetic, orth(): lax.linalg.triangular_solve(lower, matrix, left_side=False, lower=True, t...  16 us
    dot_general x1, matrix products, gram_items(): partial_gram = jnp.einsum('sxyz,swyz->sxw', block, block, precision=HIGH)  10.9 us
    dot_general x1, matrix products, local(): core_block = jnp.einsum('xr,sxyz->sryz', factor, fibres, precision=HIGH)  10.8 us
  transfers between devices with their start and end apart: 1, of which 1 were waited for; matrix products, arithmetic and copies ran while one was open for 0% of the time, Pallas kernels for 0%

commit v1 on v0

v1 whole, which is shorter than its diff:
```python
import jax
import jax.numpy as jnp
from jax import lax
from jax.experimental import pallas as pl
from jax.experimental.pallas import tpu as pltpu
from jax.sharding import PartitionSpec as P

HIGH = lax.Precision.HIGHEST
F32 = jnp.float32
BF16 = jnp.bfloat16
VMEM_BYTES = 56 << 20
ROWS_BY_ROWS = (((1,), (1,)), ((), ()))


def split(value):
    high = value.astype(BF16)
    low = (value - high.astype(F32)).astype(BF16)
    return high, low


def pack(field, rows):
    ns, nx, ny, nz = field.shape
    depth = 64

    def kernel(in_ref, out_ref):
        for block in range(depth // rows):
            out_ref[block, 0] = jnp.swapaxes(in_ref[0, :, block * rows : (block + 1) * rows, :], 0, 1)

    return pl.pallas_call(
        kernel,
        grid=(ny // depth, ns),
        out_shape=jax.ShapeDtypeStruct((ny // rows, ns, rows, nx, nz), F32),
        in_specs=[pl.BlockSpec((1, nx, depth, nz), lambda y, s: (s, 0, y, 0))],
        out_specs=pl.BlockSpec((depth // rows, 1, rows, nx, nz), lambda y, s: (y, s, 0, 0, 0)),
        compiler_params=pltpu.CompilerParams(vmem_limit_bytes=VMEM_BYTES),
        name="pack",
    )(field)


def gram(fibres):
    nb, ns, ny, nx, nz = fibres.shape
    order = nb * nx

    def kernel(in_ref, out_ref, total):
        step = pl.program_id(0)
        parts = [split(in_ref[:, 0, y].reshape(order, nz)) for y in range(ny)]
        high = jnp.concatenate([part[0] for part in parts], axis=1)
        low = jnp.concatenate([part[1] for part in parts], axis=1)
        square = lax.dot_general(high, high, ROWS_BY_ROWS, preferred_element_type=F32)
        cross = lax.dot_general(high, low, ROWS_BY_ROWS, preferred_element_type=F32)

        @pl.when(step == 0)
        def _():
            total[0] = square
            total[1] = cross

        @pl.when(step > 0)
        def _():
            total[0] += square
            total[1] += cross

        @pl.when(step == ns - 1)
        def _():
            out_ref[...] = total[0] + (total[1] + total[1].T)

    return pl.pallas_call(
        kernel,
        grid=(ns,),
        out_shape=jax.ShapeDtypeStruct((order, order), F32),
        in_specs=[pl.BlockSpec((nb, 1, ny, nx, nz), lambda s: (0, s, 0, 0, 0))],
        out_specs=pl.BlockSpec((order, order), lambda s: (0, 0)),
        scratch_shapes=[pltpu.VMEM((2, order, order), F32)],
        compiler_params=pltpu.CompilerParams(vmem_limit_bytes=VMEM_BYTES),
        name="gram",
    )(fibres)


def sum_everywhere(partial):
    n, m = partial.shape
    nb = lax.axis_size("yz")
    np_ = lax.axis_size("sp")
    rows = lax.all_to_all(partial.reshape(nb, n // nb, m), "yz", 0, 0, tiled=True)
    rows = jnp.sum(rows, axis=0)
    near, across, far = [
        lax.ppermute(rows, "sp", [(i, (i + step) % np_) for i in range(np_)])
        for step in range(1, np_)
    ]
    rows = (rows + across) + (near + far)
    copies = jnp.broadcast_to(rows[None], (nb, n // nb, m))
    return lax.all_to_all(copies, "yz", 0, 0, tiled=True).reshape(n, m)


def orth_rows(rows, count):
    square = lax.dot_general(rows, rows, ROWS_BY_ROWS, precision=HIGH, preferred_element_type=F32)
    index = lax.broadcasted_iota(jnp.int32, (count, 1), 0)
    for j in range(count):
        pivot_row = square[j : j + 1, :]
        data_row = rows[j : j + 1, :]
        scale = lax.rsqrt(square[j : j + 1, j : j + 1])
        column = jnp.where(index > j, square[:, j : j + 1] * (scale * scale), 0.0)
        square = square - column * pivot_row
        rows = rows - column * data_row
        rows = jnp.where(index == j, data_row * scale, rows)
    return rows


def iterate(gram_matrix, start_rows):
    count, order = start_rows.shape

    def kernel(gram_ref, start_ref, out_ref):
        whole = gram_ref[...]
        rows = jnp.dot(start_ref[...], whole, precision=HIGH, preferred_element_type=F32)
        rows = orth_rows(rows, count)
        rows = jnp.dot(rows, whole, precision=HIGH, preferred_element_type=F32)
        out_ref[...] = orth_rows(rows, count)

    return pl.pallas_call(
        kernel,
        out_shape=jax.ShapeDtypeStruct((count, order), F32),
        compiler_params=pltpu.CompilerParams(vmem_limit_bytes=VMEM_BYTES),
        name="iterate",
    )(gram_matrix, start_rows)


def project(fibres, factor_rows):
    nb, ns, ny, nx, nz = fibres.shape
    order = nb * nx
    count = factor_rows.shape[0]

    def kernel(in_ref, factor_ref, out_ref):
        high_rows, low_rows = split(factor_ref[...])
        both = jnp.concatenate([high_rows, low_rows], axis=0)
        for y in range(ny):
            high, low = split(in_ref[:, 0, y].reshape(order, nz))
            first = jnp.dot(both, high, preferred_element_type=F32)
            second = jnp.dot(high_rows, low, preferred_element_type=F32)
            out_ref[:, y, :] = first[:count] + (first[count:] + second)

    return pl.pallas_call(
        kernel,
        grid=(ns,),
        out_shape=jax.ShapeDtypeStruct((ns, count, ny, nz), F32),
        in_specs=[
            pl.BlockSpec((nb, 1, ny, nx, nz), lambda s: (0, s, 0, 0, 0)),
            pl.BlockSpec((count, order), lambda s: (0, 0)),
        ],
        out_specs=pl.BlockSpec((None, count, ny, nz), lambda s: (s, 0, 0, 0)),
        compiler_params=pltpu.CompilerParams(vmem_limit_bytes=VMEM_BYTES),
        name="project",
    )(fibres, factor_rows)


def local(field, start):
    nb = lax.axis_size("yz")
    blocks = pack(field, field.shape[2] // nb)
    fibres = lax.all_to_all(blocks, "yz", split_axis=0, concat_axis=0, tiled=True)
    total = sum_everywhere(gram(fibres))
    factor_rows = iterate(total, start.T)
    core_block = project(fibres, factor_rows)
    return (core_block, factor_rows.T)


def solution(mesh):
    in_specs = (P("sp", "yz", None, None), P())
    out_specs = (P("sp", None, "yz", None), P())
    return jax.shard_map(local, mesh=mesh, in_specs=in_specs, out_specs=out_specs, check_vma=False)
```

time: 393 us -> 244 us (0.62)
  waiting for transfers between devices: 141 us -> 2.28 us
  Pallas kernels: 0 us -> 56.2 us
  other arithmetic: 35.1 us -> 0.04 us
  blocking collectives: 150 us -> 179 us
  local copies, waits for them, and re-layouts: 26 us -> 0.02 us
  matrix products: 25.4 us -> 0 us
  between operations: 14.2 us -> 0.64 us
  starting transfers between devices: 0.04 us -> 4.27 us
    psum x1 -> x0, waiting for transfers between devices: 141 us -> none  [local(): gram = lax.psum(local_gram, ('yz', 'sp'))]
    pallas_call x0 -> x4, Pallas kernels: none -> 56.2 us  [the longest x1 19.4 us: iterate(): pl.pallas_call(kernel, out_shape=jax.ShapeDtypeStruct((count, order), F32...]
    another operation x10 -> x0, other arithmetic: 35.1 us -> none  [the longest x6 19.1 us: orth(): lower = jnp.linalg.cholesky(square)]
    all_to_all x1 -> x3, blocking collectives: 150 us -> 179 us  [the longest x1 150 us: local(): lax.all_to_all(blocks, 'yz', split_axis=0, concat_axis=0, tiled=True)]
    unnamed x8 -> x0, local copies, waits for them, and re-layouts: 25.9 us -> none
    dot_general x6 -> x0, matrix products: 24.9 us -> none  [the longest x1 10.9 us: gram_items(): partial_gram = jnp.einsum('sxyz,swyz->sxw', block, block, precision=HIGH)]
    ppermute x0 -> x3, starting transfers between devices: none -> 4.27 us  [sum_everywhere(): lax.ppermute(rows, 'sp', [(i, (i + step) % np_) for i in range(np_)])]
  transfers between devices with their start and end apart: 1 -> 3, of which waited for: 1 -> 2; matrix products, arithmetic and copies ran while one was open for 0% -> 0% of each run, Pallas kernels for 0% -> 0%
where the time goes in v1:
time: 244 us; the launch traced here: 243 us
  blocking collectives  179 us (73%)
  Pallas kernels  56.2 us (23%)
  starting transfers between devices  4.27 us (2%)
    all_to_all x1, blocking collectives, local(): lax.all_to_all(blocks, 'yz', split_axis=0, concat_axis=0, tiled=True)  150 us
    pallas_call x1, Pallas kernels, iterate(): pl.pallas_call(kernel, out_shape=jax.ShapeDtypeStruct((count, order), F32...  19.4 us
    pallas_call x1, Pallas kernels, pack(): pl.pallas_call(kernel, grid=(ny // depth, ns), out_shape=jax.ShapeDtypeSt...  18 us
    all_to_all x1, blocking collectives, sum_everywhere(): lax.all_to_all(partial.reshape(nb, n // nb, m), 'yz', 0, 0, tiled=True)  15 us
    all_to_all x1, blocking collectives, sum_everywhere(): return lax.all_to_all(copies, 'yz', 0, 0, tiled=True).reshape(n, m)  14 us
    pallas_call x1, Pallas kernels, project(): pl.pallas_call(kernel, grid=(ns,), out_shape=jax.ShapeDtypeStruct((ns, co...  9.73 us
    pallas_call x1, Pallas kernels, gram(): pl.pallas_call(kernel, grid=(ns,), out_shape=jax.ShapeDtypeStruct((order,...  9.16 us
  transfers between devices with their start and end apart: 3, of which 2 were waited for; matrix products, arithmetic and copies ran while one was open for 0% of the time, Pallas kernels for 0%

profile of v1, /device:TPU:1, one launch (start us, length us, event | category | flops | bytes accessed | tf_op | source)
XLA Modules:
  0.0 243.0 jit_solution(14154246420872444686)
XLA Ops:
  0.6 18.0 %pack.1 = f32[32,6,8,8,256]{4,3,2,1,0:T(8,128)} custom-call(f32[6,8,256,256]{3,2,1,0:T(8,128)} %in_ref.1), custom_call_target="tpu_custom_call" | custom-call | tf_op jit(solution)/shard_map/pack/pallas_call | solution.py:29
  18.6 150.5 %all_to_all.15.in_ref = f32[32,6,8,8,256]{4,3,2,1,0:T(8,128)} all-to-all(f32[32,6,8,8,256]{4,3,2,1,0:T(8,128)} %pack.1), channel_id=1, replica_groups=mesh['yz'=32,'sp'=4] {'yz'}, dimensions={0} | all-to-all | bytes 25165824 | tf_op jit(solution)/shard_map/all_to_all | solution.py:156
  169.1 9.2 %gram.1 = f32[256,256]{1,0:T(8,128)} custom-call(f32[32,6,8,8,256]{4,3,2,1,0:T(8,128)} %all_to_all.15.in_ref), custom_call_target="tpu_custom_call" | custom-call | tf_op jit(solution)/shard_map/gram/pallas_call | solution.py:66
  178.2 15.0 %all_to_all.16 = f32[32,8,256]{2,1,0:T(8,128)S(1)} all-to-all(f32[32,8,256]{2,1,0:T(8,128)} %bitcast.4), channel_id=1, replica_groups=mesh['yz'=32,'sp'=4] {'yz'}, dimensions={0} | all-to-all | bytes 524288 | tf_op jit(solution)/shard_map/all_to_all | solution.py:82
  193.3 2.5 %collective-permute-start.2 = (f32[8,256]{1,0:T(8,128)S(1)}, f32[8,256]{1,0:T(8,128)S(1)}, u32[]{:S(2)}, u32[]{:S(2)}) collective-permute-start(f32[8,256]{1,0:T(8,128)S(1)} %reduce_sum.9), channel_id=1, source_target_pairs={{0,3},{1,0},{2,1},{3,2},{4,7},{5,4},{6,5},{7,6},{8,11},{9,8},{10,9... | collective-permute-start | bytes 24584 | tf_op jit(solution)/shard_map/ppermute | solution.py:85
  195.8 0.0 collective-permute-start.1
  195.8 1.7 collective-permute-start
  197.6 0.0 collective-permute-done.2
  197.6 2.0 collective-permute-done.1
  199.5 0.3 collective-permute-done
  199.9 14.0 %all_to_all.17 = f32[32,8,256]{2,1,0:T(8,128)} all-to-all(f32[32,8,256]{2,1,0:T(8,128)S(1)} %broadcast_in_dim.2), channel_id=1, replica_groups=mesh['yz'=32,'sp'=4] {'yz'}, dimensions={0} | all-to-all | bytes 524288 | tf_op jit(solution)/shard_map/all_to_all | solution.py:90
  213.9 19.4 %iterate.1.factor_ref = f32[96,256]{1,0:T(8,128)} custom-call(f32[256,256]{1,0:T(8,128)} %bitcast.5, f32[96,256]{1,0:T(8,128)} %bitcast.7), custom_call_target="tpu_custom_call" | custom-call | tf_op jit(solution)/shard_map/iterate/pallas_call | solution.py:117
  233.2 9.7 %project.1 = f32[6,96,8,256]{3,2,1,0:T(8,128)} custom-call(f32[32,6,8,8,256]{4,3,2,1,0:T(8,128)} %all_to_all.15.in_ref, f32[96,256]{1,0:T(8,128)} %iterate.1.factor_ref), custom_call_target="tpu_custom_call" | custom-call | tf_op jit(solution)/shard_map/project/pallas_call | solution.py:139
  (3 shorter events, 0.1 us)
Async XLA Ops:
  193.3 4.3 %collective-permute-start.2 = (f32[8,256]{1,0:T(8,128)S(1)}, f32[8,256]{1,0:T(8,128)S(1)}, u32[]{:S(2)}, u32[]{:S(2)}) collective-permute-start(f32[8,256]{1,0:T(8,128)S(1)} %reduce_sum.9), channel_id=1, source_target_pairs={{0,3},{1,0},{2,1},{3,2},{4,7},{5,4},{6,5},{7,6},{8,11},{9,8},{10,9... | collective-permute-start | bytes 24584 | tf_op jit(solution)/shard_map/ppermute | solution.py:85
  195.8 3.7 %collective-permute-start.1 = (f32[8,256]{1,0:T(8,128)S(1)}, f32[8,256]{1,0:T(8,128)S(1)}, u32[]{:S(2)}, u32[]{:S(2)}) collective-permute-start(f32[8,256]{1,0:T(8,128)S(1)} %reduce_sum.9), channel_id=1, source_target_pairs={{0,1},{1,2},{2,3},{3,0},{4,5},{5,6},{6,7},{7,4},{8,9},{9,10},{10,1... | collective-permute-start | bytes 24584 | tf_op jit(solution)/shard_map/ppermute | solution.py:85
  195.8 4.0 %collective-permute-start = (f32[8,256]{1,0:T(8,128)S(1)}, f32[8,256]{1,0:T(8,128)S(1)}, u32[]{:S(2)}, u32[]{:S(2)}) collective-permute-start(f32[8,256]{1,0:T(8,128)S(1)} %reduce_sum.9), channel_id=1, source_target_pairs={{0,2},{1,3},{2,0},{3,1},{4,6},{5,7},{6,4},{7,5},{8,10},{9,11},{10,... | collective-permute-start | bytes 24584 | tf_op jit(solution)/shard_map/ppermute | solution.py:85

commit v2 on v1

v2 whole, which is shorter than its diff:
```python
import jax
import jax.numpy as jnp
from jax import lax
from jax.experimental import pallas as pl
from jax.experimental.pallas import tpu as pltpu
from jax.sharding import PartitionSpec as P

HIGH = lax.Precision.HIGHEST
F32 = jnp.float32
BF16 = jnp.bfloat16
LANES = 128
ROWS_BY_ROWS = (((1,), (1,)), ((), ()))


def split(value):
    high = value.astype(BF16)
    low = (value - high.astype(F32)).astype(BF16)
    return high, low


def pack(field, rows):
    ns, nx, ny, nz = field.shape
    depth = 256

    def kernel(in_ref, out_ref):
        for block in range(depth // rows):
            out_ref[block, 0] = jnp.swapaxes(in_ref[0, :, block * rows : (block + 1) * rows, :], 0, 1)

    return pl.pallas_call(
        kernel,
        grid=(ny // depth, ns),
        out_shape=jax.ShapeDtypeStruct((ny // rows, ns, rows, nx, nz), F32),
        in_specs=[pl.BlockSpec((1, nx, depth, nz), lambda y, s: (s, 0, y, 0))],
        out_specs=pl.BlockSpec((depth // rows, 1, rows, nx, nz), lambda y, s: (y, s, 0, 0, 0)),
        compiler_params=pltpu.CompilerParams(vmem_limit_bytes=40 << 20),
        name="pack",
    )(field)


def gram(fibres):
    nb, ns, ny, nx, nz = fibres.shape
    order = nb * nx

    def kernel(in_ref, out_ref, terms_ref, total):
        step = pl.program_id(0)
        highs, lows = [], []
        for y in range(ny):
            high, low = split(in_ref[:, 0, y].reshape(order, nz))
            terms_ref[0, 0, y] = high
            terms_ref[1, 0, y] = low
            highs.append(high)
            lows.append(low)
        high = jnp.concatenate(highs, axis=1)
        low = jnp.concatenate(lows, axis=1)
        square = lax.dot_general(high, high, ROWS_BY_ROWS, preferred_element_type=F32)
        cross = lax.dot_general(high, low, ROWS_BY_ROWS, preferred_element_type=F32)

        @pl.when(step == 0)
        def _():
            total[0] = square
            total[1] = cross

        @pl.when(step > 0)
        def _():
            total[0] += square
            total[1] += cross

        @pl.when(step == ns - 1)
        def _():
            out_ref[...] = total[0] + (total[1] + total[1].T)

    return pl.pallas_call(
        kernel,
        grid=(ns,),
        out_shape=(
            jax.ShapeDtypeStruct((order, order), F32),
            pltpu.HBM((2, ns, ny, order, nz), BF16),
        ),
        in_specs=[pl.BlockSpec((nb, 1, ny, nx, nz), lambda s: (0, s, 0, 0, 0))],
        out_specs=(
            pl.BlockSpec((order, order), lambda s: (0, 0)),
            pl.BlockSpec((2, 1, ny, order, nz), lambda s: (0, s, 0, 0, 0)),
        ),
        scratch_shapes=[pltpu.VMEM((2, order, order), F32)],
        compiler_params=pltpu.CompilerParams(vmem_limit_bytes=24 << 20),
        name="gram",
    )(fibres)


def sum_everywhere(partial):
    n, m = partial.shape
    nb = lax.axis_size("yz")
    np_ = lax.axis_size("sp")
    rows = lax.all_to_all(partial.reshape(nb, n // nb, m), "yz", 0, 0, tiled=True)
    rows = jnp.sum(rows, axis=0)
    near, across, far = [
        lax.ppermute(rows, "sp", [(i, (i + step) % np_) for i in range(np_)])
        for step in range(1, np_)
    ]
    rows = (rows + across) + (near + far)
    copies = jnp.broadcast_to(rows[None], (nb, n // nb, m))
    return lax.all_to_all(copies, "yz", 0, 0, tiled=True).reshape(n, m)


def eliminate(square, rows, put, size=8):
    count, width = rows.shape
    halves = width // LANES
    spread = lambda value: jnp.broadcast_to(value, (size, LANES))
    left = [
        [square[t : t + size]] + [rows[t : t + size, h * LANES : (h + 1) * LANES] for h in range(halves)]
        for t in range(0, count, size)
    ]
    for block in range(count // size):
        first = block * size
        rest = range(block + 1, count // size)
        pivots = [[spread(part[i : i + 1]) for part in left[block]] for i in range(size)]
        entry = [
            [spread(pivots[i][0][:, first + j : first + j + 1]) for j in range(i + 1)] for i in range(size)
        ]
        columns = [{t: spread(left[t][0][:, first + j : first + j + 1]) for t in rest} for j in range(size)]
        factor = [[None] * size for _ in range(size)]
        inverse = [None] * size
        for j in range(size):
            inverse[j] = 1.0 / entry[j][j]
            for i in range(j + 1, size):
                factor[i][j] = entry[i][j] * inverse[j]
            for i in range(j + 1, size):
                for m in range(j + 1, i + 1):
                    entry[i][m] = entry[i][m] - factor[i][j] * entry[m][j]
        for i in range(size):
            for j in range(i):
                pivots[i] = [a - factor[i][j] * b for a, b in zip(pivots[i], pivots[j])]
                for t in rest:
                    columns[i][t] = columns[i][t] - factor[i][j] * columns[j][t]
            scale = lax.rsqrt(entry[i][i])
            for h in range(halves):
                put(first + i, h, (pivots[i][1 + h] * scale)[0:1])
        for t in rest:
            for i in range(size):
                multiple = columns[i][t] * inverse[i]
                left[t] = [a - multiple * b for a, b in zip(left[t], pivots[i])]


def finish(gram_matrix, start_rows, terms):
    count, order = start_rows.shape
    _, ns, ny, _, nz = terms.shape

    def kernel(gram_ref, start_ref, terms_ref, core_ref, factor_ref, held, made, in_sems, out_sems):
        def arrival(s):
            return pltpu.make_async_copy(terms_ref.at[:, s], held.at[:, s], in_sems.at[s])

        def leaving(s):
            return pltpu.make_async_copy(made.at[s], core_ref.at[s], out_sems.at[s])

        for s in range(ns):
            arrival(s).start()

        def orth(rows, out_ref):
            rows = rows * lax.rsqrt(jnp.sum(rows * rows, axis=1, keepdims=True))
            square = lax.dot_general(rows, rows, ROWS_BY_ROWS, precision=HIGH, preferred_element_type=F32)
            square = jnp.concatenate([square, jnp.zeros((count, LANES - count), F32)], axis=1)

            def put(i, h, value):
                out_ref[i : i + 1, h * LANES : (h + 1) * LANES] = value

            eliminate(square, rows, put)

        whole = gram_ref[...]
        factor_ref[...] = start_ref[...]

        def step(index, carry):
            orth(jnp.dot(factor_ref[...], whole, precision=HIGH, preferred_element_type=F32), factor_ref)
            return carry

        lax.fori_loop(0, 2, step, 0)

        high_rows, low_rows = split(factor_ref[...])
        both = jnp.concatenate([high_rows, low_rows], axis=0)

        def species(s, carry):
            arrival(s).wait()
            results = []
            for y in range(ny):
                main = jnp.dot(both, held[0, s, y], preferred_element_type=F32)
                more = jnp.dot(high_rows, held[1, s, y], preferred_element_type=F32)
                results.append(main[:count] + (main[count:] + more))
            made[s] = jnp.swapaxes(jnp.stack(results), 0, 1)
            leaving(s).start()
            return carry

        lax.fori_loop(0, ns, species, 0)
        for s in range(ns):
            leaving(s).wait()

    whole_vmem = pl.BlockSpec(memory_space=pltpu.VMEM)
    anywhere = pl.BlockSpec(memory_space=pl.ANY)
    return pl.pallas_call(
        kernel,
        out_shape=(
            jax.ShapeDtypeStruct((ns, count, ny, nz), F32),
            jax.ShapeDtypeStruct((count, order), F32),
        ),
        in_specs=[whole_vmem, whole_vmem, anywhere],
        out_specs=(anywhere, whole_vmem),
        scratch_shapes=[
            pltpu.VMEM((2, ns, ny, order, nz), BF16),
            pltpu.VMEM((ns, count, ny, nz), F32),
            pltpu.SemaphoreType.DMA((ns,)),
            pltpu.SemaphoreType.DMA((ns,)),
        ],
        compiler_params=pltpu.CompilerParams(vmem_limit_bytes=56 << 20),
        name="finish",
    )(gram_matrix, start_rows, terms)


def local(field, start):
    nb = lax.axis_size("yz")
    blocks = pack(field, field.shape[2] // nb)
    fibres = lax.all_to_all(blocks, "yz", split_axis=0, concat_axis=0, tiled=True)
    partial, terms = gram(fibres)
    total = sum_everywhere(partial)
    core_block, factor_rows = finish(total, start.T, terms)
    return (core_block, factor_rows.T)


def solution(mesh):
    in_specs = (P("sp", "yz", None, None), P())
    out_specs = (P("sp", None, "yz", None), P())
    return jax.shard_map(local, mesh=mesh, in_specs=in_specs, out_specs=out_specs, check_vma=False)
```

time: 244 us -> 216 us (0.89)
  Pallas kernels: 56.2 us -> 29.1 us
    pallas_call x3 -> x2, Pallas kernels: 38.2 us -> 21.8 us  [the longest x1 13.8 us: finish(): pl.pallas_call(kernel, out_shape=(jax.ShapeDtypeStruct((ns, count, ny, nz...]
    pallas_call x1, Pallas kernels: 18 us -> 7.28 us  [pack(): pl.pallas_call(kernel, grid=(ny // depth, ns), out_shape=jax.ShapeDtypeSt...]
where the time goes in v2:
time: 216 us; the launch traced here: 215 us
  blocking collectives  179 us (83%)
  Pallas kernels  29.1 us (13%)
  starting transfers between devices  4.27 us (2%)
  waiting for transfers between devices  2.27 us (1%)
    all_to_all x1, blocking collectives, local(): lax.all_to_all(blocks, 'yz', split_axis=0, concat_axis=0, tiled=True)  150 us
    all_to_all x1, blocking collectives, sum_everywhere(): lax.all_to_all(partial.reshape(nb, n // nb, m), 'yz', 0, 0, tiled=True)  14.8 us
    all_to_all x1, blocking collectives, sum_everywhere(): return lax.all_to_all(copies, 'yz', 0, 0, tiled=True).reshape(n, m)  14 us
    pallas_call x1, Pallas kernels, finish(): pl.pallas_call(kernel, out_shape=(jax.ShapeDtypeStruct((ns, count, ny, nz...  13.8 us
    pallas_call x1, Pallas kernels, gram(): pl.pallas_call(kernel, grid=(ns,), out_shape=(jax.ShapeDtypeStruct((order...  7.96 us
    pallas_call x1, Pallas kernels, pack(): pl.pallas_call(kernel, grid=(ny // depth, ns), out_shape=jax.ShapeDtypeSt...  7.28 us
  transfers between devices with their start and end apart: 3, of which 2 were waited for; matrix products, arithmetic and copies ran while one was open for 0% of the time, Pallas kernels for 0%

profile of v2, /device:TPU:1, one launch (start us, length us, event | category | flops | bytes accessed | tf_op | source)
XLA Modules:
  0.0 215.3 jit_solution(8300431409104285135)
XLA Ops:
  0.6 7.3 %pack.1 = f32[32,6,8,8,256]{4,3,2,1,0:T(8,128)S(1)} custom-call(f32[6,8,256,256]{3,2,1,0:T(8,128)} %in_ref.1), custom_call_target="tpu_custom_call" | custom-call | tf_op jit(solution)/shard_map/pack/pallas_call | solution.py:29
  7.9 150.2 %all_to_all.15.in_ref = f32[32,6,8,8,256]{4,3,2,1,0:T(8,128)S(1)} all-to-all(f32[32,6,8,8,256]{4,3,2,1,0:T(8,128)S(1)} %pack.1), channel_id=1, replica_groups=mesh['yz'=32,'sp'=4] {'yz'}, dimensions={0} | all-to-all | bytes 25165824 | tf_op jit(solution)/shard_map/all_to_all | solution.py:219
  158.1 8.0 %gram.1 = (f32[256,256]{1,0:T(8,128)S(1)}, bf16[2,6,8,256,256]{4,3,2,1,0:T(8,128)(2,1)}) custom-call(f32[32,6,8,8,256]{4,3,2,1,0:T(8,128)S(1)} %all_to_all.15.in_ref), custom_call_target="tpu_custom_call" | custom-call | tf_op jit(solution)/shard_map/gram/pallas_call | solution.py:72
  166.0 14.8 %all_to_all.16 = f32[32,8,256]{2,1,0:T(8,128)S(1)} all-to-all(f32[32,8,256]{2,1,0:T(8,128)S(1)} %bitcast.4), channel_id=1, replica_groups=mesh['yz'=32,'sp'=4] {'yz'}, dimensions={0} | all-to-all | bytes 524288 | tf_op jit(solution)/shard_map/all_to_all | solution.py:94
  180.9 2.5 %collective-permute-start.2 = (f32[8,256]{1,0:T(8,128)S(1)}, f32[8,256]{1,0:T(8,128)S(1)}, u32[]{:S(2)}, u32[]{:S(2)}) collective-permute-start(f32[8,256]{1,0:T(8,128)S(1)} %reduce_sum.9), channel_id=1, source_target_pairs={{0,3},{1,0},{2,1},{3,2},{4,7},{5,4},{6,5},{7,6},{8,11},{9,8},{10,9... | collective-permute-start | bytes 24584 | tf_op jit(solution)/shard_map/ppermute | solution.py:97
  183.4 0.0 collective-permute-start.1
  183.4 1.7 collective-permute-start
  185.2 0.0 collective-permute-done.2
  185.2 2.0 collective-permute-done.1
  187.1 0.3 collective-permute-done
  187.5 14.0 %all_to_all.17 = f32[32,8,256]{2,1,0:T(8,128)} all-to-all(f32[32,8,256]{2,1,0:T(8,128)S(1)} %broadcast_in_dim.2), channel_id=1, replica_groups=mesh['yz'=32,'sp'=4] {'yz'}, dimensions={0} | all-to-all | bytes 524288 | tf_op jit(solution)/shard_map/all_to_all | solution.py:102
  201.5 13.8 %finish.1 = (f32[6,96,8,256]{3,2,1,0:T(8,128)}, f32[96,256]{1,0:T(8,128)}) custom-call(f32[256,256]{1,0:T(8,128)} %bitcast.5, f32[96,256]{1,0:T(8,128)} %bitcast.6, bf16[2,6,8,256,256]{4,3,2,1,0:T(8,128)(2,1)} %get-tuple-element.7.terms_ref), custom_call_target="tpu_custom_call" | custom-call | tf_op jit(solution)/shard_map/finish/pallas_call | solution.py:197
  (3 shorter events, 0.1 us)
Async XLA Ops:
  180.9 4.3 %collective-permute-start.2 = (f32[8,256]{1,0:T(8,128)S(1)}, f32[8,256]{1,0:T(8,128)S(1)}, u32[]{:S(2)}, u32[]{:S(2)}) collective-permute-start(f32[8,256]{1,0:T(8,128)S(1)} %reduce_sum.9), channel_id=1, source_target_pairs={{0,3},{1,0},{2,1},{3,2},{4,7},{5,4},{6,5},{7,6},{8,11},{9,8},{10,9... | collective-permute-start | bytes 24584 | tf_op jit(solution)/shard_map/ppermute | solution.py:97
  183.4 3.7 %collective-permute-start.1 = (f32[8,256]{1,0:T(8,128)S(1)}, f32[8,256]{1,0:T(8,128)S(1)}, u32[]{:S(2)}, u32[]{:S(2)}) collective-permute-start(f32[8,256]{1,0:T(8,128)S(1)} %reduce_sum.9), channel_id=1, source_target_pairs={{0,1},{1,2},{2,3},{3,0},{4,5},{5,6},{6,7},{7,4},{8,9},{9,10},{10,1... | collective-permute-start | bytes 24584 | tf_op jit(solution)/shard_map/ppermute | solution.py:97
  183.4 4.0 %collective-permute-start = (f32[8,256]{1,0:T(8,128)S(1)}, f32[8,256]{1,0:T(8,128)S(1)}, u32[]{:S(2)}, u32[]{:S(2)}) collective-permute-start(f32[8,256]{1,0:T(8,128)S(1)} %reduce_sum.9), channel_id=1, source_target_pairs={{0,2},{1,3},{2,0},{3,1},{4,6},{5,7},{6,4},{7,5},{8,10},{9,11},{10,... | collective-permute-start | bytes 24584 | tf_op jit(solution)/shard_map/ppermute | solution.py:97

commit v3 on v2

--- a/solution.py
+++ b/solution.py
@@ -20,18 +20,32 @@
 
 def pack(field, rows):
     ns, nx, ny, nz = field.shape
-    depth = 256
-
-    def kernel(in_ref, out_ref):
-        for block in range(depth // rows):
-            out_ref[block, 0] = jnp.swapaxes(in_ref[0, :, block * rows : (block + 1) * rows, :], 0, 1)
+
+    def kernel(in_ref, out_ref, held, in_sems):
+        def arrival(s):
+            return pltpu.make_async_copy(in_ref.at[s], held.at[s], in_sems.at[s])
+
+        for s in range(ns):
+            arrival(s).start()
+
+        def species(s, carry):
+            arrival(s).wait()
+
+            for block in range(ny // rows):
+                out_ref[block, s] = jnp.swapaxes(held[s, :, block * rows : (block + 1) * rows, :], 0, 1)
+            return carry
+
+        lax.fori_loop(0, ns, species, 0)
 
     return pl.pallas_call(
         kernel,
-        grid=(ny // depth, ns),
-        out_shape=jax.ShapeDtypeStruct((ny // rows, ns, rows, nx, nz), F32),
-        in_specs=[pl.BlockSpec((1, nx, depth, nz), lambda y, s: (s, 0, y, 0))],
-        out_specs=pl.BlockSpec((depth // rows, 1, rows, nx, nz), lambda y, s: (y, s, 0, 0, 0)),
+        out_shape=pltpu.VMEM((ny // rows, ns, rows, nx, nz), F32),
+        in_specs=[pl.BlockSpec(memory_space=pl.ANY)],
+        out_specs=pl.BlockSpec(memory_space=pltpu.VMEM),
+        scratch_shapes=[
+            pltpu.VMEM((ns, nx, ny, nz), F32),
+            pltpu.SemaphoreType.DMA((ns,)),
+        ],
         compiler_params=pltpu.CompilerParams(vmem_limit_bytes=40 << 20),
         name="pack",
     )(field)
@@ -41,48 +55,43 @@
     nb, ns, ny, nx, nz = fibres.shape
     order = nb * nx
 
-    def kernel(in_ref, out_ref, terms_ref, total):
-        step = pl.program_id(0)
-        highs, lows = [], []
-        for y in range(ny):
-            high, low = split(in_ref[:, 0, y].reshape(order, nz))
-            terms_ref[0, 0, y] = high
-            terms_ref[1, 0, y] = low
-            highs.append(high)
-            lows.append(low)
-        high = jnp.concatenate(highs, axis=1)
-        low = jnp.concatenate(lows, axis=1)
-        square = lax.dot_general(high, high, ROWS_BY_ROWS, preferred_element_type=F32)
-        cross = lax.dot_general(high, low, ROWS_BY_ROWS, preferred_element_type=F32)
-
-        @pl.when(step == 0)
-        def _():
-            total[0] = square
-            total[1] = cross
-
-        @pl.when(step > 0)
-        def _():
-            total[0] += square
-            total[1] += cross
-
-        @pl.when(step == ns - 1)
-        def _():
-            out_ref[...] = total[0] + (total[1] + total[1].T)
+    def kernel(in_ref, out_ref, terms_ref, held, total, sems):
+        def leaving(s):
+            return pltpu.make_async_copy(held.at[:, s], terms_ref.at[:, s], sems.at[s])
+
+        total[...] = jnp.zeros_like(total)
+
+        def halve(s):
+            for y in range(ny):
+                held[0, s, y], held[1, s, y] = split(in_ref[:, s, y].reshape(order, nz))
+            leaving(s).start()
+
+        halve(0)
+        for s in range(ns):
+            if s + 1 < ns:
+                halve(s + 1)
+            high = jnp.concatenate([held[0, s, y] for y in range(ny)], axis=1)
+            low = jnp.concatenate([held[1, s, y] for y in range(ny)], axis=1)
+            total[0] += lax.dot_general(high, high, ROWS_BY_ROWS, preferred_element_type=F32)
+            total[1] += lax.dot_general(high, low, ROWS_BY_ROWS, preferred_element_type=F32)
+        out_ref[...] = total[0] + (total[1] + total[1].T)
+        for s in range(ns):
+            leaving(s).wait()
 
     return pl.pallas_call(
         kernel,
-        grid=(ns,),
         out_shape=(
             jax.ShapeDtypeStruct((order, order), F32),
             pltpu.HBM((2, ns, ny, order, nz), BF16),
         ),
-        in_specs=[pl.BlockSpec((nb, 1, ny, nx, nz), lambda s: (0, s, 0, 0, 0))],
-        out_specs=(
-            pl.BlockSpec((order, order), lambda s: (0, 0)),
-            pl.BlockSpec((2, 1, ny, order, nz), lambda s: (0, s, 0, 0, 0)),
-        ),
-        scratch_shapes=[pltpu.VMEM((2, order, order), F32)],
-        compiler_params=pltpu.CompilerParams(vmem_limit_bytes=24 << 20),
+        in_specs=[pl.BlockSpec(memory_space=pltpu.VMEM)],
+        out_specs=(pl.BlockSpec(memory_space=pltpu.VMEM), pl.BlockSpec(memory_space=pl.ANY)),
+        scratch_shapes=[
+            pltpu.VMEM((2, ns, ny, order, nz), BF16),
+            pltpu.VMEM((2, order, order), F32),
+            pltpu.SemaphoreType.DMA((ns,)),
+        ],
+        compiler_params=pltpu.CompilerParams(vmem_limit_bytes=30 << 20),
         name="gram",
     )(fibres)
 

time: 216 us -> 211 us (0.977)
  Pallas kernels: 29.1 us -> 24.1 us
    pallas_call x2, Pallas kernels: 15.2 us -> 10.3 us  [the longest x1 5.2 us: gram(): pl.pallas_call(kernel, out_shape=(jax.ShapeDtypeStruct((order, order), F3...]
where the time goes in v3:
time: 211 us; the launch traced here: 210 us
  blocking collectives  179 us (85%)
  Pallas kernels  24.1 us (11%)
  starting transfers between devices  4.27 us (2%)
  waiting for transfers between devices  2.28 us (1%)
    all_to_all x1, blocking collectives, local(): lax.all_to_all(blocks, 'yz', split_axis=0, concat_axis=0, tiled=True)  150 us
    all_to_all x1, blocking collectives, sum_everywhere(): lax.all_to_all(partial.reshape(nb, n // nb, m), 'yz', 0, 0, tiled=True)  14.8 us
    all_to_all x1, blocking collectives, sum_everywhere(): return lax.all_to_all(copies, 'yz', 0, 0, tiled=True).reshape(n, m)  14 us
    pallas_call x1, Pallas kernels, finish(): pl.pallas_call(kernel, out_shape=(jax.ShapeDtypeStruct((ns, count, ny, nz...  13.8 us
    pallas_call x1, Pallas kernels, gram(): pl.pallas_call(kernel, out_shape=(jax.ShapeDtypeStruct((order, order), F3...  5.2 us
    pallas_call x1, Pallas kernels, pack(): pl.pallas_call(kernel, out_shape=pltpu.VMEM((ny // rows, ns, rows, nx, nz...  5.09 us
    ppermute x3, starting transfers between devices, sum_everywhere(): lax.ppermute(rows, 'sp', [(i, (i + step) % np_) for i in range(np_)])  4.27 us
  transfers between devices with their start and end apart: 3, of which 2 were waited for; matrix products, arithmetic and copies ran while one was open for 0% of the time, Pallas kernels for 0%

profile of v3, /device:TPU:1, one launch (start us, length us, event | category | flops | bytes accessed | tf_op | source)
XLA Modules:
  0.0 210.4 jit_solution(12760995503254237831)
XLA Ops:
  0.6 5.1 %pack.1 = f32[32,6,8,8,256]{4,3,2,1,0:T(8,128)S(1)} custom-call(f32[6,8,256,256]{3,2,1,0:T(8,128)} %in_ref.1), custom_call_target="tpu_custom_call" | custom-call | tf_op jit(solution)/shard_map/pack/pallas_call | solution.py:40
  5.7 150.2 %all_to_all.15.in_ref = f32[32,6,8,8,256]{4,3,2,1,0:T(8,128)S(1)} all-to-all(f32[32,6,8,8,256]{4,3,2,1,0:T(8,128)S(1)} %pack.1), channel_id=1, replica_groups=mesh['yz'=32,'sp'=4] {'yz'}, dimensions={0} | all-to-all | bytes 25165824 | tf_op jit(solution)/shard_map/all_to_all | solution.py:228
  155.9 5.2 %gram.1 = (f32[256,256]{1,0:T(8,128)S(1)}, bf16[2,6,8,256,256]{4,3,2,1,0:T(8,128)(2,1)}) custom-call(f32[32,6,8,8,256]{4,3,2,1,0:T(8,128)S(1)} %all_to_all.15.in_ref), custom_call_target="tpu_custom_call" | custom-call | tf_op jit(solution)/shard_map/gram/pallas_call | solution.py:81
  161.1 14.8 %all_to_all.16 = f32[32,8,256]{2,1,0:T(8,128)S(1)} all-to-all(f32[32,8,256]{2,1,0:T(8,128)S(1)} %bitcast.4), channel_id=1, replica_groups=mesh['yz'=32,'sp'=4] {'yz'}, dimensions={0} | all-to-all | bytes 524288 | tf_op jit(solution)/shard_map/all_to_all | solution.py:103
  175.9 2.5 %collective-permute-start.2 = (f32[8,256]{1,0:T(8,128)S(1)}, f32[8,256]{1,0:T(8,128)S(1)}, u32[]{:S(2)}, u32[]{:S(2)}) collective-permute-start(f32[8,256]{1,0:T(8,128)S(1)} %reduce_sum.9), channel_id=1, source_target_pairs={{0,3},{1,0},{2,1},{3,2},{4,7},{5,4},{6,5},{7,6},{8,11},{9,8},{10,9... | collective-permute-start | bytes 24584 | tf_op jit(solution)/shard_map/ppermute | solution.py:106
  178.5 0.0 collective-permute-start.1
  178.5 1.7 collective-permute-start
  180.2 0.0 collective-permute-done.2
  180.2 2.0 collective-permute-done.1
  182.2 0.3 collective-permute-done
  182.5 14.0 %all_to_all.17 = f32[32,8,256]{2,1,0:T(8,128)} all-to-all(f32[32,8,256]{2,1,0:T(8,128)S(1)} %broadcast_in_dim.2), channel_id=1, replica_groups=mesh['yz'=32,'sp'=4] {'yz'}, dimensions={0} | all-to-all | bytes 524288 | tf_op jit(solution)/shard_map/all_to_all | solution.py:111
  196.5 13.8 %finish.1 = (f32[6,96,8,256]{3,2,1,0:T(8,128)}, f32[96,256]{1,0:T(8,128)}) custom-call(f32[256,256]{1,0:T(8,128)} %bitcast.5, f32[96,256]{1,0:T(8,128)} %bitcast.6, bf16[2,6,8,256,256]{4,3,2,1,0:T(8,128)(2,1)} %get-tuple-element.7.terms_ref), custom_call_target="tpu_custom_call" | custom-call | tf_op jit(solution)/shard_map/finish/pallas_call | solution.py:206
  (3 shorter events, 0.1 us)
Async XLA Ops:
  175.9 4.3 %collective-permute-start.2 = (f32[8,256]{1,0:T(8,128)S(1)}, f32[8,256]{1,0:T(8,128)S(1)}, u32[]{:S(2)}, u32[]{:S(2)}) collective-permute-start(f32[8,256]{1,0:T(8,128)S(1)} %reduce_sum.9), channel_id=1, source_target_pairs={{0,3},{1,0},{2,1},{3,2},{4,7},{5,4},{6,5},{7,6},{8,11},{9,8},{10,9... | collective-permute-start | bytes 24584 | tf_op jit(solution)/shard_map/ppermute | solution.py:106
  178.5 3.7 %collective-permute-start.1 = (f32[8,256]{1,0:T(8,128)S(1)}, f32[8,256]{1,0:T(8,128)S(1)}, u32[]{:S(2)}, u32[]{:S(2)}) collective-permute-start(f32[8,256]{1,0:T(8,128)S(1)} %reduce_sum.9), channel_id=1, source_target_pairs={{0,1},{1,2},{2,3},{3,0},{4,5},{5,6},{6,7},{7,4},{8,9},{9,10},{10,1... | collective-permute-start | bytes 24584 | tf_op jit(solution)/shard_map/ppermute | solution.py:106
  178.5 4.0 %collective-permute-start = (f32[8,256]{1,0:T(8,128)S(1)}, f32[8,256]{1,0:T(8,128)S(1)}, u32[]{:S(2)}, u32[]{:S(2)}) collective-permute-start(f32[8,256]{1,0:T(8,128)S(1)} %reduce_sum.9), channel_id=1, source_target_pairs={{0,2},{1,3},{2,0},{3,1},{4,6},{5,7},{6,4},{7,5},{8,10},{9,11},{10,... | collective-permute-start | bytes 24584 | tf_op jit(solution)/shard_map/ppermute | solution.py:106

commit v4 on v3

--- a/solution.py
+++ b/solution.py
@@ -74,14 +74,16 @@
             low = jnp.concatenate([held[1, s, y] for y in range(ny)], axis=1)
             total[0] += lax.dot_general(high, high, ROWS_BY_ROWS, preferred_element_type=F32)
             total[1] += lax.dot_general(high, low, ROWS_BY_ROWS, preferred_element_type=F32)
-        out_ref[...] = total[0] + (total[1] + total[1].T)
+        whole = total[0] + (total[1] + total[1].T)
+        for h in range(order // LANES):
+            out_ref[h * order : (h + 1) * order] = whole[:, h * LANES : (h + 1) * LANES]
         for s in range(ns):
             leaving(s).wait()
 
     return pl.pallas_call(
         kernel,
         out_shape=(
-            jax.ShapeDtypeStruct((order, order), F32),
+            jax.ShapeDtypeStruct((order * (order // LANES), LANES), F32),
             pltpu.HBM((2, ns, ny, order, nz), BF16),
         ),
         in_specs=[pl.BlockSpec(memory_space=pltpu.VMEM)],
@@ -98,17 +100,11 @@
 
 def sum_everywhere(partial):
     n, m = partial.shape
-    nb = lax.axis_size("yz")
-    np_ = lax.axis_size("sp")
-    rows = lax.all_to_all(partial.reshape(nb, n // nb, m), "yz", 0, 0, tiled=True)
-    rows = jnp.sum(rows, axis=0)
-    near, across, far = [
-        lax.ppermute(rows, "sp", [(i, (i + step) % np_) for i in range(np_)])
-        for step in range(1, np_)
-    ]
-    rows = (rows + across) + (near + far)
-    copies = jnp.broadcast_to(rows[None], (nb, n // nb, m))
-    return lax.all_to_all(copies, "yz", 0, 0, tiled=True).reshape(n, m)
+    everyone = ("yz", "sp")
+    size = lax.axis_size("yz") * lax.axis_size("sp")
+    parts = lax.all_to_all(partial.reshape(size, n // size, m), everyone, 0, 0, tiled=True)
+    copies = jnp.broadcast_to(jnp.sum(parts, axis=0)[None], parts.shape)
+    return lax.all_to_all(copies, everyone, 0, 0, tiled=True).reshape(n, m)
 
 
 def eliminate(square, rows, put, size=8):
@@ -174,7 +170,7 @@
 
             eliminate(square, rows, put)
 
-        whole = gram_ref[...]
+        whole = jnp.concatenate([gram_ref[h * order : (h + 1) * order] for h in range(order // LANES)], axis=1)
         factor_ref[...] = start_ref[...]
 
         def step(index, carry):

time: 211 us -> 210 us (level)
  blocking collectives: 179 us -> 185 us
  starting transfers between devices: 4.27 us -> 0 us
  waiting for transfers between devices: 2.28 us -> 0 us
    all_to_all x2, blocking collectives: 28.8 us -> 34.5 us  [the longest x1 19.2 us: sum_everywhere(): lax.all_to_all(partial.reshape(size, n // size, m), everyone, 0, 0, tiled...]
    ppermute x3 -> x0, starting transfers between devices: 4.27 us -> none  [sum_everywhere(): lax.ppermute(rows, 'sp', [(i, (i + step) % np_) for i in range(np_)])]
    ppermute x3 -> x0, waiting for transfers between devices: 2.28 us -> none  [sum_everywhere(): lax.ppermute(rows, 'sp', [(i, (i + step) % np_) for i in range(np_)])]
  transfers between devices with their start and end apart: 3 -> 0, of which waited for: 2 -> 0; matrix products, arithmetic and copies ran while one was open for 0% -> 0% of each run, Pallas kernels for 0% -> 0%
where the time goes in v4:
time: 210 us
  blocking collectives  185 us (88%)
  Pallas kernels  24.2 us (12%)
    all_to_all x1, blocking collectives, local(): lax.all_to_all(blocks, 'yz', split_axis=0, concat_axis=0, tiled=True)  150 us
    all_to_all x1, blocking collectives, sum_everywhere(): lax.all_to_all(partial.reshape(size, n // size, m), everyone, 0, 0, tiled...  19.2 us
    all_to_all x1, blocking collectives, sum_everywhere(): return lax.all_to_all(copies, everyone, 0, 0, tiled=True).reshape(n, m)  15.3 us
    pallas_call x1, Pallas kernels, finish(): pl.pallas_call(kernel, out_shape=(jax.ShapeDtypeStruct((ns, count, ny, nz...  13.8 us
    pallas_call x1, Pallas kernels, gram(): pl.pallas_call(kernel, out_shape=(jax.ShapeDtypeStruct((order * (order //...  5.23 us
    pallas_call x1, Pallas kernels, pack(): pl.pallas_call(kernel, out_shape=pltpu.VMEM((ny // rows, ns, rows, nx, nz...  5.09 us

profile of v4, /device:TPU:1, one launch (start us, length us, event | category | flops | bytes accessed | tf_op | source)
XLA Modules:
  0.0 209.7 jit_solution(15708803538353613385)
XLA Ops:
  0.6 5.1 %pack.1 = f32[32,6,8,8,256]{4,3,2,1,0:T(8,128)S(1)} custom-call(f32[6,8,256,256]{3,2,1,0:T(8,128)} %in_ref.1), custom_call_target="tpu_custom_call" | custom-call | tf_op jit(solution)/shard_map/pack/pallas_call | solution.py:40
  5.7 150.2 %all_to_all.15.in_ref = f32[32,6,8,8,256]{4,3,2,1,0:T(8,128)S(1)} all-to-all(f32[32,6,8,8,256]{4,3,2,1,0:T(8,128)S(1)} %pack.1), channel_id=1, replica_groups=mesh['yz'=32,'sp'=4] {'yz'}, dimensions={0} | all-to-all | bytes 25165824 | tf_op jit(solution)/shard_map/all_to_all | solution.py:224
  155.9 5.2 %gram.1 = (f32[512,128]{1,0:T(8,128)S(1)}, bf16[2,6,8,256,256]{4,3,2,1,0:T(8,128)(2,1)}) custom-call(f32[32,6,8,8,256]{4,3,2,1,0:T(8,128)S(1)} %all_to_all.15.in_ref), custom_call_target="tpu_custom_call" | custom-call | tf_op jit(solution)/shard_map/gram/pallas_call | solution.py:83
  161.1 19.2 %all_to_all.16 = f32[128,4,128]{2,1,0:T(4,128)S(1)} all-to-all(f32[128,4,128]{2,1,0:T(4,128)S(1)} %bitcast.4), channel_id=1, replica_groups=mesh['yz'=32,'sp'=4] {'yz','sp'}, dimensions={0} | all-to-all | bytes 524288 | tf_op jit(solution)/shard_map/all_to_all | solution.py:105
  180.3 0.1 reduce_sum.9
  180.5 15.3 %all_to_all.17 = f32[128,4,128]{2,1,0:T(4,128)} all-to-all(f32[128,4,128]{2,1,0:T(4,128)S(1)} %broadcast_in_dim.2), channel_id=1, replica_groups=mesh['yz'=32,'sp'=4] {'yz','sp'}, dimensions={0} | all-to-all | bytes 524288 | tf_op jit(solution)/shard_map/all_to_all | solution.py:107
  195.8 13.8 %finish.1 = (f32[6,96,8,256]{3,2,1,0:T(8,128)}, f32[96,256]{1,0:T(8,128)}) custom-call(f32[512,128]{1,0:T(8,128)} %bitcast.5, f32[96,256]{1,0:T(8,128)} %bitcast.6, bf16[2,6,8,256,256]{4,3,2,1,0:T(8,128)(2,1)} %get-tuple-element.7.terms_ref), custom_call_target="tpu_custom_call" | custom-call | tf_op jit(solution)/shard_map/finish/pallas_call | solution.py:202
  (1 shorter events, 0.0 us)

commit v5 on v4

--- a/solution.py
+++ b/solution.py
@@ -21,18 +21,23 @@
 def pack(field, rows):
     ns, nx, ny, nz = field.shape
 
+    parts = 4
+    depth = ny // parts
+
     def kernel(in_ref, out_ref, held, in_sems):
-        def arrival(s):
-            return pltpu.make_async_copy(in_ref.at[s], held.at[s], in_sems.at[s])
-
-        for s in range(ns):
-            arrival(s).start()
+        def arrival(s, part):
+            some = pl.ds(part * depth, depth)
+            return pltpu.make_async_copy(in_ref.at[s, :, some], held.at[s, :, some], in_sems.at[s, part])
+
+        for s in range(ns):
+            for part in range(parts):
+                arrival(s, part).start()
 
         def species(s, carry):
-            arrival(s).wait()
-
-            for block in range(ny // rows):
-                out_ref[block, s] = jnp.swapaxes(held[s, :, block * rows : (block + 1) * rows, :], 0, 1)
+            for part in range(parts):
+                arrival(s, part).wait()
+                for block in range(part * depth // rows, (part + 1) * depth // rows):
+                    out_ref[block, s] = jnp.swapaxes(held[s, :, block * rows : (block + 1) * rows, :], 0, 1)
             return carry
 
         lax.fori_loop(0, ns, species, 0)
@@ -44,7 +49,7 @@
         out_specs=pl.BlockSpec(memory_space=pltpu.VMEM),
         scratch_shapes=[
             pltpu.VMEM((ns, nx, ny, nz), F32),
-            pltpu.SemaphoreType.DMA((ns,)),
+            pltpu.SemaphoreType.DMA((ns, parts)),
         ],
         compiler_params=pltpu.CompilerParams(vmem_limit_bytes=40 << 20),
         name="pack",

time: 210 us -> 210 us (level)
  no operation moved by 1% of the time
where the time goes in v5:
time: 210 us; the launch traced here: 209 us
  blocking collectives  185 us (88%)
  Pallas kernels  23.9 us (11%)
    all_to_all x1, blocking collectives, local(): lax.all_to_all(blocks, 'yz', split_axis=0, concat_axis=0, tiled=True)  150 us
    all_to_all x1, blocking collectives, sum_everywhere(): lax.all_to_all(partial.reshape(size, n // size, m), everyone, 0, 0, tiled...  19.2 us
    all_to_all x1, blocking collectives, sum_everywhere(): return lax.all_to_all(copies, everyone, 0, 0, tiled=True).reshape(n, m)  15.3 us
    pallas_call x1, Pallas kernels, finish(): pl.pallas_call(kernel, out_shape=(jax.ShapeDtypeStruct((ns, count, ny, nz...  13.8 us
    pallas_call x1, Pallas kernels, gram(): pl.pallas_call(kernel, out_shape=(jax.ShapeDtypeStruct((order * (order //...  5.23 us
    pallas_call x1, Pallas kernels, pack(): pl.pallas_call(kernel, out_shape=pltpu.VMEM((ny // rows, ns, rows, nx, nz...  4.88 us

profile of v5, /device:TPU:1, one launch (start us, length us, event | category | flops | bytes accessed | tf_op | source)
XLA Modules:
  0.0 209.4 jit_solution(11580433412317737770)
XLA Ops:
  0.6 4.9 %pack.1 = f32[32,6,8,8,256]{4,3,2,1,0:T(8,128)S(1)} custom-call(f32[6,8,256,256]{3,2,1,0:T(8,128)} %in_ref.1), custom_call_target="tpu_custom_call" | custom-call | tf_op jit(solution)/shard_map/pack/pallas_call | solution.py:45
  5.5 150.2 %all_to_all.15.in_ref = f32[32,6,8,8,256]{4,3,2,1,0:T(8,128)S(1)} all-to-all(f32[32,6,8,8,256]{4,3,2,1,0:T(8,128)S(1)} %pack.1), channel_id=1, replica_groups=mesh['yz'=32,'sp'=4] {'yz'}, dimensions={0} | all-to-all | bytes 25165824 | tf_op jit(solution)/shard_map/all_to_all | solution.py:229
  155.7 5.2 %gram.1 = (f32[512,128]{1,0:T(8,128)S(1)}, bf16[2,6,8,256,256]{4,3,2,1,0:T(8,128)(2,1)}) custom-call(f32[32,6,8,8,256]{4,3,2,1,0:T(8,128)S(1)} %all_to_all.15.in_ref), custom_call_target="tpu_custom_call" | custom-call | tf_op jit(solution)/shard_map/gram/pallas_call | solution.py:88
  160.9 19.2 %all_to_all.16 = f32[128,4,128]{2,1,0:T(4,128)S(1)} all-to-all(f32[128,4,128]{2,1,0:T(4,128)S(1)} %bitcast.4), channel_id=1, replica_groups=mesh['yz'=32,'sp'=4] {'yz','sp'}, dimensions={0} | all-to-all | bytes 524288 | tf_op jit(solution)/shard_map/all_to_all | solution.py:110
  180.1 0.1 reduce_sum.9
  180.3 15.3 %all_to_all.17 = f32[128,4,128]{2,1,0:T(4,128)} all-to-all(f32[128,4,128]{2,1,0:T(4,128)S(1)} %broadcast_in_dim.2), channel_id=1, replica_groups=mesh['yz'=32,'sp'=4] {'yz','sp'}, dimensions={0} | all-to-all | bytes 524288 | tf_op jit(solution)/shard_map/all_to_all | solution.py:112
  195.6 13.8 %finish.1 = (f32[6,96,8,256]{3,2,1,0:T(8,128)}, f32[96,256]{1,0:T(8,128)}) custom-call(f32[512,128]{1,0:T(8,128)} %bitcast.5, f32[96,256]{1,0:T(8,128)} %bitcast.6, bf16[2,6,8,256,256]{4,3,2,1,0:T(8,128)(2,1)} %get-tuple-element.7.terms_ref), custom_call_target="tpu_custom_call" | custom-call | tf_op jit(solution)/shard_map/finish/pallas_call | solution.py:207
  (1 shorter events, 0.0 us)
